TPU v7x, 256 devices: a whole 4x4x8 slice. The times are simulated.
256 devices in a mesh: member: 8 (over z), band: 16 (over x_lo, y, core), tensor: 2 (over x_hi).
Axes of the slice: x: 4 (x_hi: 2, x_lo: 2; x = x_hi * 2 + x_lo), y: 4, z: 8, core: 2. Of those that a mesh axis runs over, the one named last changes fastest.
Arguments:
- prior_grids: bfloat16 [8, 4, 128, 128, 192], P('member', None, 'band'), may hold values from -6 to 6
- w_qkv: bfloat16 [192, 3, 192], P(None, None, 'tensor'), may hold values from -0.4375 to 0.4375
- w_out: bfloat16 [192, 192], P('tensor'), may hold values from -0.4375 to 0.4375
- w_up: bfloat16 [192, 768], P(None, 'tensor'), may hold values from -0.4375 to 0.4375
- w_down: bfloat16 [768, 192], P('tensor'), may hold values from -0.21875 to 0.21875
- head_weight: bfloat16 [192, 160], replicated, may hold values from -0.4375 to 0.4375
- pos_bias: bfloat16 [6, 128, 128], P('tensor'), may hold values from -6 to 400
- zonal_offsets: int32 [8], P('member'), may hold values from 0 to 127
- obs_index: int32 [2, 128, 128, 16], P('tensor', 'band', 'member'), may hold values from 0 to 319
- obs_count: int32 [2, 128, 128], P('tensor', 'band', 'member'), may hold values from 8 to 16
- obs_value: float32 [2, 128, 128, 16], P('tensor', 'band', 'member'), may hold values from -6 to 6
- obs_weight: float32 [2, 128, 128, 16], P('tensor', 'band', 'member'), may hold values from 1 to 30
Outputs:
- analysis: float32 [8, 4, 128, 128, 160], P(None, 'tensor', 'band', 'member')
All inputs are finite; a program needn't handle non-finite values.
Results may differ from a plain program's by a relative error of at most 0.025.
Values may be sent and summed in bfloat16 or wider, within the bound.
A program may use at most 64 MiB of HBM per device.

v0:
```python
import functools
import math

import jax
import jax.numpy as jnp
from jax import lax
from jax.experimental import pallas as pl
from jax.experimental.pallas import tpu as pltpu
from jax.sharding import PartitionSpec as P

F32 = jnp.float32
BF16 = jnp.bfloat16
MESH = pl.DeviceIdType.MESH
C = 192
FF = 768
NV = 160
NEWTON = 8
MEMBERS = 8
BANDS = 16
LOG2E = 1.4426950408889634


def nt(a, b):
    return lax.dot_general(a, b, (((1,), (1,)), ((), ())), preferred_element_type=F32)


def nn(a, b):
    return jnp.dot(a, b, preferred_element_type=F32)


def iota(shape, dim):
    return lax.broadcasted_iota(jnp.int32, shape, dim)


def onehot(cond):
    return jnp.where(cond, 1.0, 0.0).astype(BF16)


def eye(n):
    return onehot(iota((n, n), 0) == iota((n, n), 1))


def gelu(x):
    return 0.5 * x * (1.0 + lax.erf(x * 0.7071067811865476))


def forecast_kernel(
    off_ref,
    prior,
    wqkv_in,
    wout_in,
    wup_in,
    wdown_in,
    bias_in,
    head_in,
    out,
    xown,
    halo,
    wqkv,
    wout,
    wup,
    wdown,
    bias,
    head,
    wout_t,
    wup_t,
    wdown_t,
    head_t,
    biasl,
    perm,
    sendperm,
    nbuf,
    xbuf,
    kbuf,
    vbuf,
    qbuf,
    mixbuf,
    fbuf,
    sendbuf,
    local_sem,
    halo_send,
    halo_recv,
    w_send,
    w_recv,
    f_send,
    f_recv,
    a_send,
    a_recv,
    a_local,
):
    member = lax.axis_index("member")
    band = lax.axis_index("band")
    tensor = lax.axis_index("tensor")
    parity = lax.rem(band, 2)
    other = 1 - tensor
    sibling = band + 1 - 2 * parity
    far = lax.rem(band + 2 * parity - 1 + BANDS, BANDS)
    xband = lax.rem(band + BANDS // 2, BANDS)
    side = (1 - parity, parity)

    barrier = pltpu.get_barrier_semaphore()
    pl.semaphore_signal(barrier, inc=1, device_id={"band": sibling}, device_id_type=MESH)
    pl.semaphore_signal(barrier, inc=1, device_id={"band": far}, device_id_type=MESH)
    pl.semaphore_signal(
        barrier, inc=1, device_id={"band": xband, "tensor": other}, device_id_type=MESH
    )
    for k in range(1, MEMBERS):
        pl.semaphore_signal(
            barrier,
            inc=1,
            device_id={"member": lax.rem(member + k, MEMBERS)},
            device_id_type=MESH,
        )

    def part(ref, i, half, c):
        if i == 0:
            return ref.at[:, half, pl.ds(c * 48, 48)]
        if i == 1:
            return ref.at[half, :, pl.ds(c * 64, 64)]
        if i == 2:
            return ref.at[half, pl.ds(c * 48, 48)]
        if i == 3:
            return ref.at[half, pl.ds(c * 96, 96)]
        return ref.at[half, pl.ds(c * 192, 192)]

    def src_part(ref, i, c):
        if i == 0:
            return ref.at[:, pl.ds(c * 48, 48)]
        if i == 1:
            return ref.at[:, pl.ds(c * 64, 64)]
        if i == 2:
            return ref.at[pl.ds(c * 48, 48)]
        if i == 3:
            return ref.at[pl.ds(c * 96, 96)]
        return ref.at[pl.ds(c * 192, 192)]

    sources = (wqkv_in, bias_in, wout_in, wup_in, wdown_in)
    targets = (wqkv, bias, wout, wup, wdown)

    own_x = pltpu.make_async_copy(
        prior.at[0, pl.ds(2 * tensor, 2)], xown, local_sem.at[0]
    )
    own_x.start()
    locals_ = []
    for i in range(5):
        dst = targets[i].at[:, tensor] if i == 0 else targets[i].at[tensor]
        locals_.append(pltpu.make_async_copy(sources[i], dst, local_sem.at[1 + i]))
    locals_.append(pltpu.make_async_copy(head_in, head, local_sem.at[6]))
    for copy in locals_:
        copy.start()

    pl.semaphore_wait(barrier, 3 + MEMBERS - 1)

    halos = []
    for ph, peer in ((0, sibling), (1, far)):
        halos.append(
            pltpu.make_async_remote_copy(
                src_ref=prior.at[0, pl.ds(2 * tensor, 2), pl.ds(4 * side[ph], 4)],
                dst_ref=halo.at[ph],
                send_sem=halo_send.at[ph],
                recv_sem=halo_recv.at[ph],
                device_id={"band": peer},
                device_id_type=MESH,
            )
        )
    weights = []
    forwards = []
    for i in range(5):
        weights.append(
            pltpu.make_async_remote_copy(
                src_ref=src_part(sources[i], i, parity),
                dst_ref=part(targets[i], i, tensor, parity),
                send_sem=w_send.at[i],
                recv_sem=w_recv.at[i],
                device_id={"band": xband, "tensor": other},
                device_id_type=MESH,
            )
        )
        piece = part(targets[i], i, other, parity)
        forwards.append(
            pltpu.make_async_remote_copy(
                src_ref=piece,
                dst_ref=piece,
                send_sem=f_send.at[i],
                recv_sem=f_recv.at[i],
                device_id={"band": sibling},
                device_id_type=MESH,
            )
        )
    weights[0].start()
    halos[0].start()
    halos[1].start()
    for i in range(1, 5):
        weights[i].start()

    offset = off_ref[0]
    row_i = iota((256, 256), 0)
    col_i = iota((256, 256), 1)
    place = jnp.bitwise_and((row_i // 16) * 8 + jnp.bitwise_and(row_i, 7) + offset, 127)
    want = jnp.bitwise_and(row_i // 8, 1) * 128 + place
    perm[...] = onehot(want == col_i)

    def build_send(i, _):
        rows = iota((64, 1024), 0)
        cols = iota((64, 1024), 1)
        level = jnp.bitwise_and(rows // 8, 1)
        row = rows // 16
        where = jnp.bitwise_and(i * 8 + jnp.bitwise_and(rows, 7) + offset, 127)
        target = (where // 16) * 128 + level * 64 + row * 16 + jnp.bitwise_and(where, 15)
        sendperm[pl.ds(pl.multiple_of(i * 64, 64), 64), :] = onehot(target == cols)
        return 0

    lax.fori_loop(0, 16, build_send, 0)

    def prepare(block, ph, slot, keep):
        moved = nn(perm[...], block)
        mean = jnp.sum(moved, axis=1, keepdims=True) * (1.0 / C)
        center = moved - mean
        spread = jnp.sum(center * center, axis=1, keepdims=True) * (1.0 / C)
        normed = (center * lax.rsqrt(spread + 1e-05)).astype(BF16)
        nbuf[ph, :, slot] = normed.reshape(16, 16, C)
        if keep:
            xbuf[ph, :, slot] = moved.astype(BF16).reshape(16, 16, C)

    own_x.wait()
    for ph in range(2):

        def own_row(r, _, ph=ph):
            row = 4 * side[ph] + r
            block = jnp.concatenate([xown[0, row], xown[1, row]], axis=0)
            prepare(block, ph, r, True)
            return 0

        lax.fori_loop(0, 4, own_row, 0)

    for copy in locals_:
        copy.wait()
    weights[0].wait()
    forwards[0].start()
    halos[0].wait()

    def halo_rows(ph):
        def body(r, _):
            block = jnp.concatenate([halo[ph, 0, r], halo[ph, 1, r]], axis=0)
            prepare(block, ph, 4 + r, False)
            return 0

        lax.fori_loop(0, 4, body, 0)

    halo_rows(0)
    for i in range(1, 5):
        weights[i].wait()
        forwards[i].start()
    for i in range(5):
        forwards[i].wait()

    wout_t[...] = nt(eye(C), wout[...].reshape(C, C)).astype(BF16)
    for half in range(2):
        wup_t[half * 384 : half * 384 + 384, :] = nt(eye(384), wup[half]).astype(BF16)
        wdown_t[:, half * 384 : half * 384 + 384] = nt(eye(C), wdown[half]).astype(BF16)
    head_t[...] = nt(eye(NV), head[...]).astype(BF16)

    key_i = iota((128, 128), 0)
    pos_i = iota((128, 128), 1)
    edge = jnp.logical_or(band == 0, band == BANDS - 1)
    for ph in range(2):
        turn = 4 * (1 - side[ph])

        def position(index):
            row = jnp.bitwise_and(index // 16 + turn, 7)
            return (jnp.bitwise_and(index // 8, 1) * 8 + row) * 8 + jnp.bitwise_and(index, 7)

        keys_sel = onehot(position(key_i) == pos_i)
        first = onehot(jnp.logical_and(position(key_i) == pos_i, key_i < 64))
        second = onehot(jnp.logical_and(position(key_i - 64) == pos_i, key_i >= 64))
        for t in range(3):
            turned = []
            for h in (2 * t, 2 * t + 1):
                turned.append(nt(keys_sel, bias[h // 3, h % 3]).astype(BF16))
            for w in range(2):
                lo, hi = (turned[0], turned[1]) if w == 0 else (turned[1], turned[0])
                value = (nt(lo, first) + nt(hi, second)) * LOG2E
                if ph == 1:
                    value = jnp.where(jnp.logical_and(edge, key_i >= 64), -1e9, value)
                biasl[ph, w, t] = value

    lane = iota((1, 128), 1)
    low = lane < 64
    zero64 = jnp.zeros((64, 128), BF16)
    ones16 = jnp.ones((16, 128), BF16)

    def phase(ph):
        wq = wqkv[0].reshape(C, C)
        wk = wqkv[1].reshape(C, C)
        wv = wqkv[2].reshape(C, C)

        def project(j, _):
            tokens = nbuf[ph, pl.ds(4 * j, 4)].reshape(512, C)
            own = nbuf[ph, pl.ds(4 * j, 4), 0:4].reshape(256, C)
            kbuf[pl.ds(pl.multiple_of(512 * j, 512), 512), :] = nt(tokens, wk).astype(BF16)
            v = nt(wv, tokens).astype(BF16)
            for i in range(2):
                vbuf[2 * j + i] = v[:, 256 * i : 256 * i + 256]
            q = nt(wq, own)
            for i in range(2):
                qbuf[2 * j + i] = q[:, 128 * i : 128 * i + 128].astype(BF16)
            return 0

        lax.fori_loop(0, 4, project, 0)

        def window_pair(j, _):
            keys = kbuf[pl.ds(pl.multiple_of(256 * j, 256), 256), :]
            values = vbuf[j]
            queries = qbuf[j].astype(F32)
            lows = []
            highs = []
            for h in range(6):
                q = queries[32 * h : 32 * h + 32]
                if h % 2:
                    q = pltpu.roll(q, 64, 1)
                lows.append(jnp.where(low, q, 0.0).astype(BF16))
                highs.append(jnp.where(low, 0.0, q).astype(BF16))
            results = []
            for w in range(2):
                even, odd = (lows, highs) if w == 0 else (highs, lows)
                columns = []
                for t in range(3):
                    pieces = [zero64] * 3
                    pieces[t] = jnp.concatenate([even[2 * t], odd[2 * t + 1]], axis=0)
                    columns.append(jnp.concatenate(pieces, axis=0))
                stacked = jnp.concatenate(columns, axis=1)
                scores = nn(keys[128 * w : 128 * w + 128], stacked)
                result = []
                for t in range(3):
                    s = scores[:, 128 * t : 128 * t + 128] * (LOG2E * 32**-0.5)
                    s = s + biasl[ph, w, t]
                    s = s - jnp.max(s, axis=0, keepdims=True)
                    probs = jnp.exp2(s).astype(BF16)
                    left = jnp.concatenate(
                        [values[64 * t : 64 * t + 64, 128 * w : 128 * w + 128], ones16], axis=0
                    )
                    result.append(nn(left, probs))
                results.append(result)
            rows = []
            for t in range(3):
                a, b = results[0][t], results[1][t]
                even = jnp.where(low, a[0:32], b[0:32])
                even = even / jnp.where(low, a[64:65], b[64:65])
                odd = jnp.where(low, b[32:64], a[32:64])
                odd = odd / jnp.where(low, b[64:65], a[64:65])
                rows.append(even)
                rows.append(pltpu.roll(odd, 64, 1))
            mixbuf[:, pl.ds(pl.multiple_of(128 * j, 128), 128)] = jnp.concatenate(
                rows, axis=0
            ).astype(BF16)
            return 0

        lax.fori_loop(0, 8, window_pair, 0)

        def mlp(j, _):
            cols = pl.ds(pl.multiple_of(256 * j, 256), 256)
            prior_t = nt(eye(C), xbuf[ph, pl.ds(4 * j, 4)].reshape(256, C))
            one = prior_t + nn(wout_t[...], mixbuf[:, cols])
            mean = jnp.sum(one, axis=0, keepdims=True) * (1.0 / C)
            center = one - mean
            spread = jnp.sum(center * center, axis=0, keepdims=True) * (1.0 / C)
            normed = (center * lax.rsqrt(spread + 1e-05)).astype(BF16)
            active = gelu(nn(wup_t[...], normed)).astype(BF16)
            two = (one + nn(wdown_t[...], active)).astype(BF16)
            fbuf[:, cols] = nn(head_t[...], two).astype(BF16)
            return 0

        lax.fori_loop(0, 4, mlp, 0)

        sent = nn(fbuf[...], sendperm[...])
        for d in range(MEMBERS):
            sendbuf[ph, d] = sent[:, 128 * d : 128 * d + 128].astype(BF16)
        copies = []
        for k in range(1, MEMBERS):
            to = lax.rem(member + k, MEMBERS)
            copies.append(
                pltpu.make_async_remote_copy(
                    src_ref=sendbuf.at[ph, to],
                    dst_ref=out.at[ph, member],
                    send_sem=a_send.at[ph, k],
                    recv_sem=a_recv.at[ph, k],
                    device_id={"member": to},
                    device_id_type=MESH,
                )
            )
        mine = pltpu.make_async_copy(sendbuf.at[ph, member], out.at[ph, member], a_local.at[ph])
        for copy in copies:
            copy.start()
        mine.start()
        return copies + [mine]

    pending = phase(0)
    halos[1].wait()
    halo_rows(1)
    pending = pending + phase(1)
    for copy in pending:
        copy.wait()


def forecast(off, prior, wqkv, wout, wup, wdown, bias, head):
    vmem = pltpu.VMEM
    dma = pltpu.SemaphoreType.DMA
    hbm = pl.BlockSpec(memory_space=pl.ANY)
    return pl.pallas_call(
        forecast_kernel,
        out_shape=jax.ShapeDtypeStruct((2, MEMBERS, NV, 128), BF16),
        in_specs=[pl.BlockSpec(memory_space=pltpu.SMEM)] + [hbm] * 7,
        out_specs=hbm,
        scratch_shapes=[
            vmem((2, 8, 128, C), BF16),
            vmem((2, 2, 4, 128, C), BF16),
            vmem((3, 2, 96, C), BF16),
            vmem((2, 96, C), BF16),
            vmem((2, C, 384), BF16),
            vmem((2, 384, C), BF16),
            vmem((2, 3, 128, 128), BF16),
            vmem((C, NV), BF16),
            vmem((C, C), BF16),
            vmem((FF, C), BF16),
            vmem((C, FF), BF16),
            vmem((NV, C), BF16),
            vmem((2, 2, 3, 128, 128), F32),
            vmem((256, 256), BF16),
            vmem((1024, 1024), BF16),
            vmem((2, 16, 8, 16, C), BF16),
            vmem((2, 16, 4, 16, C), BF16),
            vmem((2048, C), BF16),
            vmem((8, C, 256), BF16),
            vmem((8, C, 128), BF16),
            vmem((C, 1024), BF16),
            vmem((NV, 1024), BF16),
            vmem((2, MEMBERS, NV, 128), BF16),
            dma((7,)),
            dma((2,)),
            dma((2,)),
            dma((5,)),
            dma((5,)),
            dma((5,)),
            dma((5,)),
            dma((2, MEMBERS)),
            dma((2, MEMBERS)),
            dma((2,)),
        ],
        compiler_params=pltpu.CompilerParams(
            collective_id=0, has_side_effects=True, vmem_limit_bytes=48 * 1024 * 1024
        ),
        cost_estimate=pl.CostEstimate(
            flops=3_000_000_000, bytes_accessed=6_000_000, transcendentals=3_200_000
        ),
        name="forecast",
    )(off, prior, wqkv, wout, wup, wdown, bias, head)


def analysis_kernel(recv, index, count, value, weight, out, xf, vt):
    parity = lax.rem(lax.axis_index("band"), 2)
    eye128 = eye(128)
    for ph in range(2):
        base = 4 * (1 - parity) if ph == 0 else 4 * parity
        for m in range(MEMBERS):
            x = nt(eye128, recv[ph, m])
            xf[m, :, pl.ds(base, 4), :, 0:NV] = x.reshape(2, 4, 16, NV)

    lane = iota((128, 128), 1)
    pad = jnp.zeros((128, 112), jnp.int32)
    spread_index = jnp.concatenate([index[0].reshape(128, 16), pad], axis=1)
    idx = jnp.take_along_axis(spread_index, lane // 8, axis=1, mode="promise_in_bounds")
    level = idx >= NV
    inner = jnp.where(level, idx - NV, idx)
    upper = inner >= 128
    inner = jnp.bitwise_and(inner, 127)
    slot_member = jnp.bitwise_and(lane, 7)
    observed = jnp.zeros((128, 128), F32)
    for m in range(MEMBERS):
        picks = []
        for a in range(2):
            for part in range(2):
                x = xf[m, a, :, :, 128 * part : 128 * part + 128].reshape(128, 128)
                picks.append(jnp.take_along_axis(x, inner, axis=1, mode="promise_in_bounds"))
        got = jnp.where(
            level,
            jnp.where(upper, picks[3], picks[2]),
            jnp.where(upper, picks[1], picks[0]),
        )
        observed = jnp.where(slot_member == m, got, observed)
    obs_t = observed.T

    blank = jnp.zeros((128, 96), F32)
    terms = jnp.concatenate(
        [value[0].reshape(128, 16), weight[0].reshape(128, 16), blank], axis=1
    ).T
    counts = count[0].astype(F32).astype(BF16)
    spread = onehot(iota((16, 128), 0) == jnp.bitwise_and(iota((16, 128), 1), 15))
    wide = nn(counts, spread)
    live_count = jnp.sum(
        jnp.where(iota((8, 128), 0) == iota((8, 128), 1) // 16, wide, 0.0), axis=0, keepdims=True
    )

    sub = iota((8, 128), 0)
    rows = [jnp.zeros((8, 128), F32) for _ in range(MEMBERS)]
    right = jnp.zeros((8, 128), F32)
    for k in range(16):
        y = obs_t[8 * k : 8 * k + 8]
        mean = jnp.sum(y, axis=0, keepdims=True) * (1.0 / MEMBERS)
        dev = y - mean
        r = jnp.where(live_count > k, terms[16 + k : 17 + k], 0.0)
        scaled = dev * r
        right = right + scaled * (terms[k : k + 1] - mean)
        for i in range(MEMBERS):
            rows[i] = rows[i] + scaled[i : i + 1] * dev
    for i in range(MEMBERS):
        rows[i] = rows[i] + jnp.where(sub == i, MEMBERS - 1.0, 0.0)
    diagonal = jnp.zeros((8, 128), F32)
    for i in range(MEMBERS):
        diagonal = diagonal + jnp.where(sub == i, rows[i], 0.0)
    trace = jnp.sum(diagonal, axis=0, keepdims=True)
    inverse_trace = 1.0 / trace
    g = [row * inverse_trace for row in rows]

    def product(left, right_mat):
        result = []
        for i in range(MEMBERS):
            total = left[i][0:1] * right_mat[0]
            for j in range(1, MEMBERS):
                total = total + left[i][j : j + 1] * right_mat[j]
            result.append(total)
        return result

    def factor_of(zg):
        return [jnp.where(sub == i, 1.5, 0.0) - 0.5 * zg[i] for i in range(MEMBERS)]

    f = factor_of(g)
    g = product(g, f)
    z = f
    for step in range(1, NEWTON):
        f = factor_of(product(z, g))
        if step < NEWTON - 1:
            g = product(g, f)
        z = product(f, z)

    def apply(mat, vec):
        total = mat[0] * vec[0:1]
        for j in range(1, MEMBERS):
            total = total + mat[j] * vec[j : j + 1]
        return total

    wbar = apply(z, apply(z, right)) * inverse_trace
    scale = math.sqrt(MEMBERS - 1.0) * lax.rsqrt(trace)
    full = [wbar[i : i + 1] + z[i] * scale for i in range(MEMBERS)]
    mean_row = full[0]
    for i in range(1, MEMBERS):
        mean_row = mean_row + full[i]
    shift = (1.0 - mean_row) * (1.0 / MEMBERS)
    final = jnp.concatenate([row + shift for row in full] + [jnp.zeros((64, 128), F32)], axis=0)
    vt[...] = final.T

    def update(p, _):
        row = p // 2
        half = pl.ds(pl.multiple_of(jnp.bitwise_and(p, 1) * 8, 8), 8)
        coeff = vt[pl.ds(pl.multiple_of(p * 8, 8), 8), :]
        for a in range(2):
            x = [xf[i, a, row, half, :] for i in range(MEMBERS)]
            for m in range(MEMBERS):
                total = coeff[:, m : m + 1] * x[0]
                for i in range(1, MEMBERS):
                    total = total + coeff[:, 8 * i + m : 8 * i + m + 1] * x[i]
                out[m, a, row, half, :] = total[:, 0:NV]
        return 0

    lax.fori_loop(0, 16, update, 0)


def analyse(recv, index, count, value, weight):
    return pl.pallas_call(
        analysis_kernel,
        out_shape=jax.ShapeDtypeStruct((MEMBERS, 2, 8, 16, NV), F32),
        scratch_shapes=[
            pltpu.VMEM((MEMBERS, 2, 8, 16, 256), F32),
            pltpu.VMEM((128, 128), F32),
        ],
        compiler_params=pltpu.CompilerParams(vmem_limit_bytes=48 * 1024 * 1024),
        cost_estimate=pl.CostEstimate(
            flops=20_000_000, bytes_accessed=3_000_000, transcendentals=0
        ),
        name="analyse",
    )(recv, index, count, value, weight)


def shards(
    prior_grids,
    w_qkv,
    w_out,
    w_up,
    w_down,
    head_weight,
    pos_bias,
    zonal_offsets,
    obs_index,
    obs_count,
    obs_value,
    obs_weight,
):
    recv = forecast(
        zonal_offsets,
        prior_grids,
        w_qkv.transpose(1, 2, 0),
        w_out,
        w_up,
        w_down,
        pos_bias,
        head_weight,
    )
    return analyse(recv, obs_index, obs_count, obs_value, obs_weight)


def solution(mesh):
    return jax.shard_map(
        shards,
        mesh=mesh,
        in_specs=(
            P("member", None, "band", None, None),
            P(None, None, "tensor"),
            P("tensor", None),
            P(None, "tensor"),
            P("tensor", None),
            P(),
            P("tensor", None, None),
            P("member"),
            P("tensor", "band", "member", None),
            P("tensor", "band", "member"),
            P("tensor", "band", "member", None),
            P("tensor", "band", "member", None),
        ),
        out_specs=P(None, "tensor", "band", "member", None),
        check_vma=False,
    )
```

profile of v0, /device:TPU:1, one launch (start us, length us, event | category | flops | bytes accessed | tf_op | source)
XLA Modules:
  0.0 69.3 jit_solution(8699987159614289578)
XLA Ops:
  0.7 1.0 %copy.16.head_in = bf16[192,160]{1,0:T(8,128)(2,1)S(1)} copy(bf16[192,160]{0,1:T(8,128)(2,1)} %param.17) | data formatting | bytes 122880 | tf_op args[5]
  1.6 0.0 copy-start.4
  1.7 0.0 copy-start.5
  1.7 0.0 copy-start.6
  1.7 1.1 %copy.13 = bf16[192,3,96]{0,2,1:T(8,128)(2,1)S(1)} copy(bf16[192,3,96]{2,0,1:T(8,128)(2,1)} %param.13) | data formatting | bytes 221184 | tf_op args[1]
  2.8 1.0 %copy.15.wdown_in = bf16[384,192]{1,0:T(8,128)(2,1)S(1)} copy(bf16[384,192]{0,1:T(8,128)(2,1)} %param.16) | data formatting | bytes 294912 | tf_op args[4]
  3.8 2.8 %copy.14.prior = bf16[1,4,8,128,192]{4,3,2,1,0:T(8,128)(2,1)S(1)} copy(bf16[1,4,8,128,192]{3,4,2,1,0:T(8,128)(2,1)} %param.12) | data formatting | bytes 3145728 | tf_op args[0]
  6.6 0.0 copy-done.4
  6.6 0.0 copy-done.5
  6.6 0.0 copy-done.6
  6.6 0.0 copy-start
  6.6 0.0 copy-start.1
  6.6 0.0 copy-start.2
  6.7 0.0 copy-start.3
  6.7 55.9 %forecast.1.recv = bf16[2,8,160,128]{3,2,1,0:T(8,128)(2,1)S(1)} custom-call(s32[1]{0:T(128)S(6)} %copy.17.off_ref, bf16[1,4,8,128,192]{4,3,2,1,0:T(8,128)(2,1)S(1)} %copy.14.prior, bf16[3,96,192]{2,1,0:T(8,128)(2,1)S(1)} %bitcast.1, bf16[96,192]{1,0:T(8,128)(2,1)S(1)} %copy-done.6, bf16[192,384]{1,0:T(8,128)(2,1)S(1)} %copy-done.4, ...), custom_call_target="tpu_custom_call" | custom-call | flops 3000000000 | bytes 6000000 | tf_op jit(solution)/shard_map/forecast/pallas_call | solution.py:409
  62.5 0.0 copy-done
  62.5 0.0 copy-done.1
  62.6 0.0 copy-done.2
  62.6 0.0 copy-done.3
  62.6 6.8 %analyse.1 = f32[8,2,8,16,160]{4,3,2,1,0:T(8,128)} custom-call(bf16[2,8,160,128]{3,2,1,0:T(8,128)(2,1)S(1)} %forecast.1.recv, s32[1,8,16,16]{3,2,1,0:T(8,128)S(1)} %copy-done, s32[1,8,16]{2,1,0:T(8,128)S(1)} %copy-done.3, f32[1,8,16,16]{3,2,1,0:T(8,128)S(1)} %copy-done.1, f32[1,8,16,16]{3,2,1,0:T(8,128)S(1)} %copy-done.2), custom_call_target="tpu_custom_call" | custom-call | flops 20000000 | bytes 3000000 | tf_op jit(solution)/shard_map/analyse/pallas_call | solution.py:578
Async XLA Ops:
  1.6 4.9 %copy-start.4 = (bf16[192,384]{1,0:T(8,128)(2,1)S(1)}, bf16[192,384]{1,0:T(8,128)(2,1)}, u32[]{:S(2)}) copy-start(bf16[192,384]{1,0:T(8,128)(2,1)} %wup_in.1) | copy-start | bytes 442372
  1.7 4.9 %copy-start.5 = (bf16[3,128,128]{2,1,0:T(8,128)(2,1)S(1)}, bf16[3,128,128]{2,1,0:T(8,128)(2,1)}, u32[]{:S(2)}) copy-start(bf16[3,128,128]{2,1,0:T(8,128)(2,1)} %bias_in.1) | copy-start | bytes 294916
  1.7 4.9 %copy-start.6 = (bf16[96,192]{1,0:T(8,128)(2,1)S(1)}, bf16[96,192]{1,0:T(8,128)(2,1)}, u32[]{:S(2)}) copy-start(bf16[96,192]{1,0:T(8,128)(2,1)} %wout_in.1) | copy-start | bytes 110596
  6.6 55.9 %copy-start = (s32[1,8,16,16]{3,2,1,0:T(8,128)S(1)}, s32[1,8,16,16]{3,2,1,0:T(8,128)}, u32[]{:S(2)}) copy-start(s32[1,8,16,16]{3,2,1,0:T(8,128)} %index.1) | copy-start | bytes 24580
  6.6 55.9 %copy-start.1 = (f32[1,8,16,16]{3,2,1,0:T(8,128)S(1)}, f32[1,8,16,16]{3,2,1,0:T(8,128)}, u32[]{:S(2)}) copy-start(f32[1,8,16,16]{3,2,1,0:T(8,128)} %value.1) | copy-start | bytes 24580
  6.6 55.9 %copy-start.2 = (f32[1,8,16,16]{3,2,1,0:T(8,128)S(1)}, f32[1,8,16,16]{3,2,1,0:T(8,128)}, u32[]{:S(2)}) copy-start(f32[1,8,16,16]{3,2,1,0:T(8,128)} %weight.1) | copy-start | bytes 24580
  6.7 55.9 %copy-start.3 = (s32[1,8,16]{2,1,0:T(8,128)S(1)}, s32[1,8,16]{2,1,0:T(8,128)}, u32[]{:S(2)}) copy-start(s32[1,8,16]{2,1,0:T(8,128)} %count.1) | copy-start | bytes 1540
where the time goes:
time: 69.6 us; the launch traced here: 69.3 us
  Pallas kernels  62.6 us (90%)
  local copies, waits for them, and re-layouts  5.92 us (9%)
  between operations  0.79 us (1%)
    pallas_call x1, Pallas kernels, forecast(): pl.pallas_call(forecast_kernel, out_shape=jax.ShapeDtypeStruct((2, MEMBER...  55.9 us
    pallas_call x1, Pallas kernels, analyse(): pl.pallas_call(analysis_kernel, out_shape=jax.ShapeDtypeStruct((MEMBERS,...  6.76 us
    unnamed x18, local copies, waits for them, and re-layouts  5.92 us

commit v1 on v0

v1 whole, which is shorter than its diff:
```python
import functools
import math

import jax
import jax.numpy as jnp
from jax import lax
from jax.experimental import pallas as pl
from jax.experimental.pallas import tpu as pltpu
from jax.sharding import PartitionSpec as P

F32 = jnp.float32
BF16 = jnp.bfloat16
MESH = pl.DeviceIdType.MESH
C = 192
FF = 768
NV = 160
NEWTON = 8
MEMBERS = 8
BANDS = 16
LOG2E = 1.4426950408889634


def nt(a, b):
    return lax.dot_general(a, b, (((1,), (1,)), ((), ())), preferred_element_type=F32)


def nn(a, b):
    return jnp.dot(a, b, preferred_element_type=F32)


def iota(shape, dim):
    return lax.broadcasted_iota(jnp.int32, shape, dim)


def onehot(cond):
    return jnp.where(cond, 1.0, 0.0).astype(BF16)


def eye(n):
    return onehot(iota((n, n), 0) == iota((n, n), 1))


def gelu(x):
    return 0.5 * x * (1.0 + lax.erf(x * 0.7071067811865476))


def forecast_kernel(
    off_ref,
    prior,
    wqkv_in,
    wout_in,
    wup_in,
    wdown_in,
    bias_in,
    head_in,
    out,
    xown,
    halo,
    wqkv,
    wout,
    wup,
    wdown,
    bias,
    head_t,
    wqkv_t,
    wout_t,
    wup_t,
    biasl,
    perm,
    sendperm,
    nbuf,
    xbuf,
    kbuf,
    vbuf,
    qbuf,
    sbuf,
    pbuf,
    mixbuf,
    onebuf,
    nextbuf,
    actbuf,
    fbuf,
    sendbuf,
    local_sem,
    halo_send,
    halo_recv,
    w_send,
    w_recv,
    f_send,
    f_recv,
    a_send,
    a_recv,
    a_local,
):
    member = lax.axis_index("member")
    band = lax.axis_index("band")
    tensor = lax.axis_index("tensor")
    parity = lax.rem(band, 2)
    other = 1 - tensor
    sibling = band + 1 - 2 * parity
    far = lax.rem(band + 2 * parity - 1 + BANDS, BANDS)
    xband = lax.rem(band + BANDS // 2, BANDS)
    side = (1 - parity, parity)

    barrier = pltpu.get_barrier_semaphore()
    pl.semaphore_signal(barrier, inc=1, device_id={"band": sibling}, device_id_type=MESH)
    pl.semaphore_signal(barrier, inc=1, device_id={"band": far}, device_id_type=MESH)
    pl.semaphore_signal(
        barrier, inc=1, device_id={"band": xband, "tensor": other}, device_id_type=MESH
    )
    for k in range(1, MEMBERS):
        pl.semaphore_signal(
            barrier,
            inc=1,
            device_id={"member": lax.rem(member + k, MEMBERS)},
            device_id_type=MESH,
        )

    def part(ref, i, half, c):
        if i == 0:
            return ref.at[half, :, pl.ds(c * 96, 96)]
        if i == 1:
            return ref.at[half, :, pl.ds(c * 64, 64)]
        if i == 2:
            return ref.at[half, pl.ds(c * 48, 48)]
        return ref.at[half, pl.ds(c * 96, 96)]

    def src_part(ref, i, c):
        if i == 0:
            return ref.at[:, pl.ds(c * 96, 96)]
        if i == 1:
            return ref.at[:, pl.ds(c * 64, 64)]
        if i == 2:
            return ref.at[pl.ds(c * 48, 48)]
        return ref.at[pl.ds(c * 96, 96)]

    sources = (wqkv_in, bias_in, wout_in, wup_in, wdown_in)
    targets = (wqkv, bias, wout, wup, wdown)

    own_x = pltpu.make_async_copy(
        prior.at[0, pl.ds(2 * tensor, 2)], xown, local_sem.at[0]
    )
    own_x.start()
    locals_ = []
    for i in range(5):
        locals_.append(
            pltpu.make_async_copy(sources[i], targets[i].at[tensor], local_sem.at[1 + i])
        )
    locals_.append(pltpu.make_async_copy(head_in, head_t, local_sem.at[6]))
    for copy in locals_:
        copy.start()

    offset = off_ref[0]
    row_i = iota((256, 256), 0)
    col_i = iota((256, 256), 1)
    place = jnp.bitwise_and((row_i // 16) * 8 + jnp.bitwise_and(row_i, 7) + offset, 127)
    want = jnp.bitwise_and(row_i // 8, 1) * 128 + place
    perm[...] = onehot(want == col_i)

    def build_send(i, _):
        rows = iota((64, 1024), 0)
        cols = iota((64, 1024), 1)
        level = jnp.bitwise_and(rows // 8, 1)
        row = rows // 16
        where = jnp.bitwise_and(i * 8 + jnp.bitwise_and(rows, 7) + offset, 127)
        target = (where // 16) * 128 + level * 64 + row * 16 + jnp.bitwise_and(where, 15)
        sendperm[pl.ds(pl.multiple_of(i * 64, 64), 64), :] = onehot(target == cols)
        return 0

    pl.semaphore_wait(barrier, 3 + MEMBERS - 1)

    halos = []
    for ph, peer in ((0, sibling), (1, far)):
        halos.append(
            pltpu.make_async_remote_copy(
                src_ref=prior.at[0, pl.ds(2 * tensor, 2), pl.ds(4 * side[ph], 4)],
                dst_ref=halo.at[ph],
                send_sem=halo_send.at[ph],
                recv_sem=halo_recv.at[ph],
                device_id={"band": peer},
                device_id_type=MESH,
            )
        )
    weights = []
    forwards = []
    for i in range(5):
        weights.append(
            pltpu.make_async_remote_copy(
                src_ref=src_part(sources[i], i, parity),
                dst_ref=part(targets[i], i, tensor, parity),
                send_sem=w_send.at[i],
                recv_sem=w_recv.at[i],
                device_id={"band": xband, "tensor": other},
                device_id_type=MESH,
            )
        )
        piece = part(targets[i], i, other, parity)
        forwards.append(
            pltpu.make_async_remote_copy(
                src_ref=piece,
                dst_ref=piece,
                send_sem=f_send.at[i],
                recv_sem=f_recv.at[i],
                device_id={"band": sibling},
                device_id_type=MESH,
            )
        )
    weights[0].start()
    halos[0].start()
    weights[1].start()
    halos[1].start()
    for i in range(2, 5):
        weights[i].start()

    def prepare(block, ph, slot, keep):
        tokens = block.astype(F32)
        mean = jnp.sum(tokens, axis=0, keepdims=True) * (1.0 / C)
        center = tokens - mean
        spread = jnp.sum(center * center, axis=0, keepdims=True) * (1.0 / C)
        normed = (center * lax.rsqrt(spread + 1e-05)).astype(BF16)
        nbuf[ph, :, slot] = nt(perm[...], normed).astype(BF16).reshape(16, 16, C)
        if keep:
            xbuf[ph, :, slot] = nt(perm[...], block).astype(BF16).reshape(16, 16, C)

    own_x.wait()
    for ph in range(2):
        for r in range(4):
            row = 4 * side[ph] + r
            prepare(jnp.concatenate([xown[0, row], xown[1, row]], axis=1), ph, r, True)

    def halo_rows(ph):
        for r in range(4):
            prepare(jnp.concatenate([halo[ph, 0, r], halo[ph, 1, r]], axis=1), ph, 4 + r, False)

    lax.fori_loop(0, 16, build_send, 0)
    for copy in locals_:
        copy.wait()
    weights[0].wait()
    forwards[0].start()
    halos[0].wait()
    halo_rows(0)
    weights[1].wait()
    forwards[1].start()
    forwards[0].wait()

    for half in range(2):
        for i in range(3):
            turned = nt(eye(96), wqkv[half, i]).astype(BF16)
            if i > 0:
                wqkv_t[i, half * 96 : half * 96 + 96] = turned
                continue
            for n in range(3):
                h = 3 * half + n
                to = (h // 2) * 32 + (h % 2) * 96
                wqkv_t[0, to : to + 32] = turned[32 * n : 32 * n + 32]

    lane = iota((1, 128), 1)
    low = lane < 64

    def project(ph):
        wk, wv = wqkv_t[1], wqkv_t[2]
        wq_even, wq_odd = wqkv_t[0, 0:96], wqkv_t[0, 96:192]
        wide_low = jnp.bitwise_and(iota((1, 256), 1), 127) < 64
        for j in range(4):
            tokens = nbuf[ph, 4 * j : 4 * j + 4].reshape(512, C)
            own = nbuf[ph, 4 * j : 4 * j + 4, 0:4].reshape(4, 64, C)
            swapped = jnp.concatenate([own[1], own[0], own[3], own[2]], axis=0)
            kbuf[512 * j : 512 * j + 512, :] = nt(tokens, wk).astype(BF16)
            v = nt(wv, tokens).astype(BF16)
            q = jnp.concatenate([nt(wq_even, own.reshape(256, C)), nt(wq_odd, swapped)], axis=0)
            lows = jnp.where(wide_low, q, 0.0).astype(BF16)
            highs = jnp.where(wide_low, 0.0, q).astype(BF16)
            for i in range(2):
                vbuf[2 * j + i] = v[:, 256 * i : 256 * i + 256]
                qbuf[2 * j + i, 0] = lows[:, 128 * i : 128 * i + 128]
                qbuf[2 * j + i, 1] = highs[:, 128 * i : 128 * i + 128]

    zero64 = jnp.zeros((64, 128), BF16)
    ones16 = jnp.ones((16, 128), BF16)

    def attend(ph):
        def step(i, _):
            j = jnp.clip(i - 2, 0, 7)
            results = []
            for w in range(2):
                result = []
                for t in range(3):
                    left = jnp.concatenate(
                        [vbuf[j, 64 * t : 64 * t + 64, 128 * w : 128 * w + 128], ones16], axis=0
                    )
                    result.append(nn(left, pbuf[w, :, 128 * t : 128 * t + 128]))
                results.append(result)
            where = pl.ds(pl.multiple_of(128 * j, 128), 128)
            for t in range(3):
                a, b = results[0][t], results[1][t]
                even = jnp.where(low, a[0:32], b[0:32])
                even = even * (1.0 / jnp.where(low, a[64:65], b[64:65]))
                odd = jnp.where(low, b[32:64], a[32:64])
                odd = odd * (1.0 / jnp.where(low, b[64:65], a[64:65]))
                mixbuf[32 * t : 32 * t + 32, where] = even.astype(BF16)
                mixbuf[96 + 32 * t : 128 + 32 * t, where] = odd.astype(BF16)

            for w in range(2):
                for t in range(3):
                    s = sbuf[w, :, 128 * t : 128 * t + 128] * (LOG2E * 32**-0.5)
                    s = s + biasl[ph, w, t]
                    s = s - jnp.max(s, axis=0, keepdims=True)
                    pbuf[w, :, 128 * t : 128 * t + 128] = jnp.exp2(s).astype(BF16)

            j = jnp.minimum(i, 7)
            for w in range(2):
                columns = []
                for t in range(3):
                    pieces = [zero64] * 3
                    pieces[t] = jnp.concatenate(
                        [
                            qbuf[j, w, 32 * t : 32 * t + 32],
                            qbuf[j, 1 - w, 96 + 32 * t : 128 + 32 * t],
                        ],
                        axis=0,
                    )
                    columns.append(jnp.concatenate(pieces, axis=0))
                start = pl.multiple_of(256 * j + 128 * w, 128)
                sbuf[w] = nn(kbuf[pl.ds(start, 128), :], jnp.concatenate(columns, axis=1))
            return 0

        lax.fori_loop(0, 10, step, 0)

    def mlp(ph):
        def first(j):
            cols = slice(256 * j, 256 * j + 256)
            prior_t = nt(eye(C), xbuf[ph, 4 * j : 4 * j + 4].reshape(256, C))
            odd = mixbuf[96:192, cols].astype(F32)
            odd = jnp.concatenate(
                [pltpu.roll(odd[:, 0:128], 64, 1), pltpu.roll(odd[:, 128:256], 64, 1)], axis=1
            ).astype(BF16)
            mixed = jnp.concatenate([mixbuf[0:96, cols], odd], axis=0)
            one = prior_t + nn(wout_t[...], mixed)
            onebuf[:, cols] = one
            mean = jnp.sum(one, axis=0, keepdims=True) * (1.0 / C)
            center = one - mean
            spread = jnp.sum(center * center, axis=0, keepdims=True) * (1.0 / C)
            nextbuf[:, cols] = (center * lax.rsqrt(spread + 1e-05)).astype(BF16)

        def second(j):
            cols = slice(256 * j, 256 * j + 256)
            actbuf[:, cols] = gelu(nn(wup_t[...], nextbuf[:, cols])).astype(BF16)

        def third(j):
            cols = slice(256 * j, 256 * j + 256)
            raised = nn(wdown[0], actbuf[0:384, cols]) + nn(wdown[1], actbuf[384:768, cols])
            two = (onebuf[:, cols] + raised).astype(BF16)
            fbuf[:, cols] = nn(head_t[...], two).astype(BF16)

        for j in range(6):
            if 0 <= j - 2 < 4:
                third(j - 2)
            if 0 <= j - 1 < 4:
                second(j - 1)
            if j < 4:
                first(j)

    half_member = member // 2
    odd_member = lax.rem(member, 2)

    def send(ph):
        copies = []
        for k in (2, 1, 3, 0):
            pair = lax.rem(half_member + k, 4)
            cols = pl.ds(pl.multiple_of(256 * pair, 256), 256)
            sent = nn(fbuf[...], sendperm[:, cols]).astype(BF16)
            for j in range(2):
                sendbuf[ph, 2 * pair + j] = sent[:, 128 * j : 128 * j + 128]
            for j in range(2):
                to = 2 * pair + j
                if k == 0:
                    if j == 1:
                        continue
                    to = member + 1 - 2 * odd_member
                copy = pltpu.make_async_remote_copy(
                    src_ref=sendbuf.at[ph, to],
                    dst_ref=out.at[ph, member],
                    send_sem=a_send.at[ph, 2 * k + j],
                    recv_sem=a_recv.at[ph, 2 * k + odd_member],
                    device_id={"member": to},
                    device_id_type=MESH,
                )
                copy.start()
                copies.append(copy)
        mine = pltpu.make_async_copy(sendbuf.at[ph, member], out.at[ph, member], a_local.at[ph])
        mine.start()
        return copies, mine

    def finish(ph, copies, mine):
        for copy in copies:
            copy.wait_send()
        mine.wait()
        for k in (2, 1, 3, 0):
            for j in range(2):
                origin = 2 * lax.rem(half_member + 4 - k, 4) + j
                slot = 2 * k + j
                if k == 0:
                    if j == 1:
                        continue
                    origin = member + 1 - 2 * odd_member
                    slot = 1 - odd_member
                pltpu.make_async_remote_copy(
                    src_ref=sendbuf.at[ph, origin],
                    dst_ref=out.at[ph, origin],
                    send_sem=a_send.at[ph, slot],
                    recv_sem=a_recv.at[ph, slot],
                    device_id={"member": origin},
                    device_id_type=MESH,
                ).wait_recv()

    project(0)
    for i in range(2, 5):
        weights[i].wait()
        forwards[i].start()
    forwards[1].wait()

    key_i = iota((128, 128), 0)
    pos_i = iota((128, 128), 1)

    def position(index):
        return (
            jnp.bitwise_and(index // 8, 1) * 8 + jnp.bitwise_and(index // 16, 7)
        ) * 8 + jnp.bitwise_and(index, 7)

    natural = onehot(position(key_i) == pos_i)
    crossed = onehot(position(jnp.bitwise_xor(key_i, 64)) == pos_i)
    edge = jnp.logical_or(band == 0, band == BANDS - 1)
    straight = []
    swapped = []
    for h in range(6):
        turned = nt(natural, bias[h // 3, h % 3]).astype(BF16)
        straight.append(nt(turned, natural) * LOG2E)
        swapped.append(nt(turned, crossed) * LOG2E)
    for t in range(3):
        for w in range(2):
            lo, hi = (2 * t, 2 * t + 1) if w == 0 else (2 * t + 1, 2 * t)
            upper = jnp.where(low, straight[lo], swapped[hi])
            lower = jnp.where(low, swapped[lo], straight[hi])
            lower = jnp.concatenate([lower[64:128], lower[0:64]], axis=0)
            first_side = side[0] == 1
            biasl[0, w, t] = jnp.where(first_side, upper, lower)
            second = jnp.where(first_side, lower, upper)
            biasl[1, w, t] = jnp.where(jnp.logical_and(edge, key_i >= 64), -1e9, second)

    attend(0)
    for i in range(2, 5):
        forwards[i].wait()
    heads_in = [wout[h // 3, 32 * (h % 3) : 32 * (h % 3) + 32] for h in (0, 2, 4, 1, 3, 5)]
    wout_t[...] = nt(eye(C), jnp.concatenate(heads_in, axis=0)).astype(BF16)
    for half in range(2):
        wup_t[half * 384 : half * 384 + 384, :] = nt(eye(384), wup[half]).astype(BF16)
    mlp(0)
    first_sent = send(0)
    halos[1].wait()
    halo_rows(1)
    project(1)
    attend(1)
    mlp(1)
    second_sent = send(1)
    finish(0, *first_sent)
    finish(1, *second_sent)


def forecast(off, prior, wqkv, wout, wup, wdown, bias, head):
    vmem = pltpu.VMEM
    dma = pltpu.SemaphoreType.DMA
    hbm = pl.BlockSpec(memory_space=pl.ANY)
    return pl.pallas_call(
        forecast_kernel,
        out_shape=jax.ShapeDtypeStruct((2, MEMBERS, NV, 128), BF16),
        in_specs=[pl.BlockSpec(memory_space=pltpu.SMEM)] + [hbm] * 7,
        out_specs=hbm,
        scratch_shapes=[
            vmem((2, 8, C, 128), BF16),
            vmem((2, 2, 4, C, 128), BF16),
            vmem((2, 3, C, 96), BF16),
            vmem((2, 96, C), BF16),
            vmem((2, C, 384), BF16),
            vmem((2, C, 384), BF16),
            vmem((2, 3, 128, 128), BF16),
            vmem((NV, C), BF16),
            vmem((3, C, C), BF16),
            vmem((C, C), BF16),
            vmem((FF, C), BF16),
            vmem((2, 2, 3, 128, 128), F32),
            vmem((256, 256), BF16),
            vmem((1024, 1024), BF16),
            vmem((2, 16, 8, 16, C), BF16),
            vmem((2, 16, 4, 16, C), BF16),
            vmem((2048, C), BF16),
            vmem((8, C, 256), BF16),
            vmem((8, 2, C, 128), BF16),
            vmem((2, 128, 384), F32),
            vmem((2, 128, 384), BF16),
            vmem((C, 1024), BF16),
            vmem((C, 1024), F32),
            vmem((C, 1024), BF16),
            vmem((FF, 1024), BF16),
            vmem((NV, 1024), BF16),
            vmem((2, MEMBERS, NV, 128), BF16),
            dma((7,)),
            dma((2,)),
            dma((2,)),
            dma((5,)),
            dma((5,)),
            dma((5,)),
            dma((5,)),
            dma((2, MEMBERS)),
            dma((2, MEMBERS)),
            dma((2,)),
        ],
        compiler_params=pltpu.CompilerParams(
            collective_id=0, has_side_effects=True, vmem_limit_bytes=60 * 1024 * 1024
        ),
        cost_estimate=pl.CostEstimate(
            flops=3_000_000_000, bytes_accessed=6_000_000, transcendentals=3_200_000
        ),
        name="forecast",
    )(off, prior, wqkv, wout, wup, wdown, bias, head)


def analysis_kernel(recv, index, count, value, weight, out, xf, vt, ybuf):
    parity = lax.rem(lax.axis_index("band"), 2)
    eye128 = eye(128)
    for ph in range(2):
        base = 4 * (1 - parity) if ph == 0 else 4 * parity
        for m in range(MEMBERS):
            x = nt(eye128, recv[ph, m])
            xf[m, :, pl.ds(base, 4), :, 0:NV] = x.reshape(2, 4, 16, NV)

    lane = iota((128, 128), 1)
    pad = jnp.zeros((128, 112), jnp.int32)
    spread_index = jnp.concatenate([index[0].reshape(128, 16), pad], axis=1)
    idx = jnp.take_along_axis(spread_index, lane // 8, axis=1, mode="promise_in_bounds")
    level = idx >= NV
    inner = jnp.where(level, idx - NV, idx)
    upper = inner >= 128
    inner = jnp.bitwise_and(inner, 127)
    slot_member = jnp.bitwise_and(lane, 7)
    observed = jnp.zeros((128, 128), F32)
    for m in range(MEMBERS):
        picks = []
        for a in range(2):
            for part in range(2):
                x = xf[m, a, :, :, 128 * part : 128 * part + 128].reshape(128, 128)
                picks.append(jnp.take_along_axis(x, inner, axis=1, mode="promise_in_bounds"))
        got = jnp.where(
            level,
            jnp.where(upper, picks[3], picks[2]),
            jnp.where(upper, picks[1], picks[0]),
        )
        observed = jnp.where(slot_member == m, got, observed)
    obs_t = observed.T

    blank = jnp.zeros((128, 96), F32)
    terms = jnp.concatenate(
        [value[0].reshape(128, 16), weight[0].reshape(128, 16), blank], axis=1
    ).T
    counts = count[0].astype(F32).astype(BF16)
    spread = onehot(iota((16, 128), 0) == jnp.bitwise_and(iota((16, 128), 1), 15))
    wide = nn(counts, spread)
    live_count = jnp.sum(
        jnp.where(iota((8, 128), 0) == iota((8, 128), 1) // 16, wide, 0.0), axis=0, keepdims=True
    )

    sub = iota((8, 128), 0)
    rows = [jnp.zeros((8, 128), F32) for _ in range(MEMBERS)]
    right = jnp.zeros((8, 128), F32)
    for k in range(16):
        y = obs_t[8 * k : 8 * k + 8]
        mean = jnp.sum(y, axis=0, keepdims=True) * (1.0 / MEMBERS)
        dev = y - mean
        r = jnp.where(live_count > k, terms[16 + k : 17 + k], 0.0)
        scaled = dev * r
        right = right + scaled * (terms[k : k + 1] - mean)
        for i in range(MEMBERS):
            rows[i] = rows[i] + scaled[i : i + 1] * dev
    for i in range(MEMBERS):
        rows[i] = rows[i] + jnp.where(sub == i, MEMBERS - 1.0, 0.0)
    diagonal = jnp.zeros((8, 128), F32)
    for i in range(MEMBERS):
        diagonal = diagonal + jnp.where(sub == i, rows[i], 0.0)
    trace = jnp.sum(diagonal, axis=0, keepdims=True)
    inverse_trace = 1.0 / trace
    g = [row * inverse_trace for row in rows]

    def product(left, right_mat):
        result = []
        for i in range(MEMBERS):
            total = left[i][0:1] * right_mat[0]
            for j in range(1, MEMBERS):
                total = total + left[i][j : j + 1] * right_mat[j]
            result.append(total)
        return result

    def factor_of(zg):
        return [jnp.where(sub == i, 1.5, 0.0) - 0.5 * zg[i] for i in range(MEMBERS)]

    f = factor_of(g)
    g = product(g, f)
    z = f
    for step in range(1, NEWTON):
        f = factor_of(product(z, g))
        if step < NEWTON - 1:
            g = product(g, f)
        z = product(f, z)

    def apply(mat, vec):
        total = mat[0] * vec[0:1]
        for j in range(1, MEMBERS):
            total = total + mat[j] * vec[j : j + 1]
        return total

    wbar = apply(z, apply(z, right)) * inverse_trace
    scale = math.sqrt(MEMBERS - 1.0) * lax.rsqrt(trace)
    full = [wbar[i : i + 1] + z[i] * scale for i in range(MEMBERS)]
    mean_row = full[0]
    for i in range(1, MEMBERS):
        mean_row = mean_row + full[i]
    shift = (1.0 - mean_row) * (1.0 / MEMBERS)
    low = iota((1, 128), 1) < 64
    for i in range(MEMBERS):
        value_i = full[i] + shift
        turned = pltpu.roll(value_i, 64, 1)
        first = jnp.where(low, value_i, turned)
        second = jnp.where(low, turned, value_i)
        vt[0, i] = jnp.where(parity == 1, first, second)
        vt[1, i] = jnp.where(parity == 1, second, first)

    def update(n, _):
        at = pl.ds(pl.multiple_of(n * 16, 16), 16)
        for ph in range(2):
            x = [recv[ph, i, at, :].astype(F32) for i in range(MEMBERS)]
            for m in range(MEMBERS):
                total = vt[ph, 0, m : m + 1, :] * x[0]
                for i in range(1, MEMBERS):
                    total = total + vt[ph, i, m : m + 1, :] * x[i]
                high = total.astype(BF16)
                ybuf[0, ph, m, at, :] = high
                ybuf[1, ph, m, at, :] = (total - high.astype(F32)).astype(BF16)
        return 0

    lax.fori_loop(0, NV // 16, update, 0)

    for ph in range(2):
        base = 4 * (1 - parity) if ph == 0 else 4 * parity
        for m in range(MEMBERS):
            x = nt(eye128, ybuf[0, ph, m]) + nt(eye128, ybuf[1, ph, m])
            out[m, :, pl.ds(base, 4), :, :] = x.reshape(2, 4, 16, NV)


def analyse(recv, index, count, value, weight):
    return pl.pallas_call(
        analysis_kernel,
        out_shape=jax.ShapeDtypeStruct((MEMBERS, 2, 8, 16, NV), F32),
        scratch_shapes=[
            pltpu.VMEM((MEMBERS, 2, 8, 16, 256), F32),
            pltpu.VMEM((2, MEMBERS, MEMBERS, 128), F32),
            pltpu.VMEM((2, 2, MEMBERS, NV, 128), BF16),
        ],
        compiler_params=pltpu.CompilerParams(vmem_limit_bytes=48 * 1024 * 1024),
        cost_estimate=pl.CostEstimate(
            flops=20_000_000, bytes_accessed=3_000_000, transcendentals=0
        ),
        name="analyse",
    )(recv, index, count, value, weight)


def shards(
    prior_grids,
    w_qkv,
    w_out,
    w_up,
    w_down,
    head_weight,
    pos_bias,
    zonal_offsets,
    obs_index,
    obs_count,
    obs_value,
    obs_weight,
):
    recv = forecast(
        zonal_offsets,
        prior_grids.transpose(0, 1, 2, 4, 3),
        w_qkv.transpose(1, 0, 2),
        w_out,
        w_up,
        w_down.T,
        pos_bias,
        head_weight.T,
    )
    return analyse(recv, obs_index, obs_count, obs_value, obs_weight)


def solution(mesh):
    return jax.shard_map(
        shards,
        mesh=mesh,
        in_specs=(
            P("member", None, "band", None, None),
            P(None, None, "tensor"),
            P("tensor", None),
            P(None, "tensor"),
            P("tensor", None),
            P(),
            P("tensor", None, None),
            P("member"),
            P("tensor", "band", "member", None),
            P("tensor", "band", "member"),
            P("tensor", "band", "member", None),
            P("tensor", "band", "member", None),
        ),
        out_specs=P(None, "tensor", "band", "member", None),
        check_vma=False,
    )
```

time: 69.6 us -> 49.7 us (0.71)
  Pallas kernels: 62.6 us -> 47.7 us
  local copies, waits for them, and re-layouts: 5.92 us -> 1.1 us
    pallas_call x1, Pallas kernels: 55.9 us -> 42 us  [forecast(): pl.pallas_call(forecast_kernel, out_shape=jax.ShapeDtypeStruct((2, MEMBER...]
    unnamed x18 -> x10, local copies, waits for them, and re-layouts: 5.92 us -> 1.1 us
    pallas_call x1, Pallas kernels: 6.76 us -> 5.72 us  [analyse(): pl.pallas_call(analysis_kernel, out_shape=jax.ShapeDtypeStruct((MEMBERS,...]
where the time goes in v1:
time: 49.7 us; the launch traced here: 49.5 us
  Pallas kernels  47.7 us (96%)
  local copies, waits for them, and re-layouts  1.1 us (2%)
  between operations  0.73 us (1%)
    pallas_call x1, Pallas kernels, forecast(): pl.pallas_call(forecast_kernel, out_shape=jax.ShapeDtypeStruct((2, MEMBER...  42 us
    pallas_call x1, Pallas kernels, analyse(): pl.pallas_call(analysis_kernel, out_shape=jax.ShapeDtypeStruct((MEMBERS,...  5.72 us
    unnamed x10, local copies, waits for them, and re-layouts  1.1 us

profile of v1, /device:TPU:1, one launch (start us, length us, event | category | flops | bytes accessed | tf_op | source)
XLA Modules:
  0.0 49.5 jit_solution(2435570900457382251)
XLA Ops:
  0.7 0.0 copy-start.1
  0.7 0.0 copy-start.2
  0.7 0.0 copy-start.3
  0.7 0.0 copy-start.4
  0.7 42.0 %forecast.1.recv = bf16[2,8,160,128]{3,2,1,0:T(8,128)(2,1)} custom-call(s32[1]{0:T(128)S(6)} %copy.13.off_ref, bf16[1,4,8,192,128]{4,3,2,1,0:T(8,128)(2,1)} %bitcast.4, bf16[3,192,96]{2,1,0:T(8,128)(2,1)} %bitcast.5, bf16[96,192]{1,0:T(8,128)(2,1)} %wout_in.1, bf16[192,384]{1,0:T(8,128)(2,1)} %wup_in.1, bf16[192,384]{1,0:T(8,128)(2,1)} %bitcast.6, ...), custom_call_target="tpu_custom_call" | custom-call | flops 3000000000 | bytes 6000000 | tf_op jit(solution)/shard_map/forecast/pallas_call | solution.py:473
  42.7 0.0 copy-done.1
  42.7 0.0 copy-done.2
  42.7 0.0 copy-done.3
  42.7 0.0 copy-done.4
  42.7 0.0 copy-start
  42.7 1.1 %copy-done = bf16[2,8,160,128]{3,2,1,0:T(8,128)(2,1)S(1)} copy-done((bf16[2,8,160,128]{3,2,1,0:T(8,128)(2,1)S(1)}, bf16[2,8,160,128]{3,2,1,0:T(8,128)(2,1)}, u32[]{:S(2)}) %copy-start) | copy-done | bytes 655384
  43.8 5.7 %analyse.1 = f32[8,2,8,16,160]{4,3,2,1,0:T(8,128)} custom-call(bf16[2,8,160,128]{3,2,1,0:T(8,128)(2,1)S(1)} %copy-done, s32[1,8,16,16]{3,2,1,0:T(8,128)S(1)} %copy-done.1, s32[1,8,16]{2,1,0:T(8,128)S(1)} %copy-done.4, f32[1,8,16,16]{3,2,1,0:T(8,128)S(1)} %copy-done.2, f32[1,8,16,16]{3,2,1,0:T(8,128)S(1)} %copy-done.3), custom_call_target="tpu_custom_call" | custom-call | flops 20000000 | bytes 3000000 | tf_op jit(solution)/shard_map/analyse/pallas_call | solution.py:658
Async XLA Ops:
  0.7 42.0 %copy-start.1 = (s32[1,8,16,16]{3,2,1,0:T(8,128)S(1)}, s32[1,8,16,16]{3,2,1,0:T(8,128)}, u32[]{:S(2)}) copy-start(s32[1,8,16,16]{3,2,1,0:T(8,128)} %index.1) | copy-start | bytes 24580
  0.7 42.0 %copy-start.2 = (f32[1,8,16,16]{3,2,1,0:T(8,128)S(1)}, f32[1,8,16,16]{3,2,1,0:T(8,128)}, u32[]{:S(2)}) copy-start(f32[1,8,16,16]{3,2,1,0:T(8,128)} %value.1) | copy-start | bytes 24580
  0.7 42.0 %copy-start.3 = (f32[1,8,16,16]{3,2,1,0:T(8,128)S(1)}, f32[1,8,16,16]{3,2,1,0:T(8,128)}, u32[]{:S(2)}) copy-start(f32[1,8,16,16]{3,2,1,0:T(8,128)} %weight.1) | copy-start | bytes 24580
  0.7 42.0 %copy-start.4 = (s32[1,8,16]{2,1,0:T(8,128)S(1)}, s32[1,8,16]{2,1,0:T(8,128)}, u32[]{:S(2)}) copy-start(s32[1,8,16]{2,1,0:T(8,128)} %count.1) | copy-start | bytes 1540
  42.7 1.1 %copy-start = (bf16[2,8,160,128]{3,2,1,0:T(8,128)(2,1)S(1)}, bf16[2,8,160,128]{3,2,1,0:T(8,128)(2,1)}, u32[]{:S(2)}) copy-start(bf16[2,8,160,128]{3,2,1,0:T(8,128)(2,1)} %forecast.1.recv) | copy-start | bytes 1966084

commit v2 on v1

--- a/solution.py
+++ b/solution.py
@@ -278,7 +278,7 @@
     zero64 = jnp.zeros((64, 128), BF16)
     ones16 = jnp.ones((16, 128), BF16)
 
-    def attend(ph):
+    def attend(ph, begin, end):
         def step(i, _):
             j = jnp.clip(i - 2, 0, 7)
             results = []
@@ -324,7 +324,7 @@
                 sbuf[w] = nn(kbuf[pl.ds(start, 128), :], jnp.concatenate(columns, axis=1))
             return 0
 
-        lax.fori_loop(0, 10, step, 0)
+        lax.fori_loop(begin, end, step, 0)
 
     def mlp(ph):
         def first(j):
@@ -354,6 +354,8 @@
 
         for j in range(6):
             if 0 <= j - 2 < 4:
+                if ph == 0 and j == 2:
+                    forwards[4].wait()
                 third(j - 2)
             if 0 <= j - 1 < 4:
                 second(j - 1)
@@ -447,11 +449,11 @@
             second = jnp.where(first_side, lower, upper)
             biasl[1, w, t] = jnp.where(jnp.logical_and(edge, key_i >= 64), -1e9, second)
 
-    attend(0)
-    for i in range(2, 5):
-        forwards[i].wait()
+    attend(0, 0, 10)
+    forwards[2].wait()
     heads_in = [wout[h // 3, 32 * (h % 3) : 32 * (h % 3) + 32] for h in (0, 2, 4, 1, 3, 5)]
     wout_t[...] = nt(eye(C), jnp.concatenate(heads_in, axis=0)).astype(BF16)
+    forwards[3].wait()
     for half in range(2):
         wup_t[half * 384 : half * 384 + 384, :] = nt(eye(384), wup[half]).astype(BF16)
     mlp(0)
@@ -459,7 +461,7 @@
     halos[1].wait()
     halo_rows(1)
     project(1)
-    attend(1)
+    attend(1, 0, 10)
     mlp(1)
     second_sent = send(1)
     finish(0, *first_sent)
@@ -474,7 +476,7 @@
         forecast_kernel,
         out_shape=jax.ShapeDtypeStruct((2, MEMBERS, NV, 128), BF16),
         in_specs=[pl.BlockSpec(memory_space=pltpu.SMEM)] + [hbm] * 7,
-        out_specs=hbm,
+        out_specs=pl.BlockSpec(memory_space=pl.ANY),
         scratch_shapes=[
             vmem((2, 8, C, 128), BF16),
             vmem((2, 2, 4, C, 128), BF16),
@@ -524,36 +526,68 @@
     )(off, prior, wqkv, wout, wup, wdown, bias, head)
 
 
-def analysis_kernel(recv, index, count, value, weight, out, xf, vt, ybuf):
+def analysis_kernel(
+    arrived,
+    index_in,
+    count_in,
+    value_in,
+    weight_in,
+    out,
+    recv,
+    index,
+    count,
+    value,
+    weight,
+    in_sem,
+    xf,
+    vt,
+    ybuf,
+    obuf,
+    work,
+    scaled_ref,
+    out_sem,
+):
     parity = lax.rem(lax.axis_index("band"), 2)
+    loads = []
+    for ph in range(2):
+        load = pltpu.make_async_copy(arrived.at[ph], recv.at[ph], in_sem.at[ph])
+        load.start()
+        loads.append(load)
+    observations = []
+    for n, (src, dst) in enumerate(
+        ((index_in, index), (count_in, count), (value_in, value), (weight_in, weight))
+    ):
+        load = pltpu.make_async_copy(src, dst, in_sem.at[2 + n])
+        load.start()
+        observations.append(load)
     eye128 = eye(128)
+    fold = onehot(jnp.bitwise_and(iota((64, 128), 1), 63) == iota((64, 128), 0))
+    low_level = onehot(iota((1, 128), 1) < 64)
+    high_level = onehot(iota((1, 128), 1) >= 64)
     for ph in range(2):
         base = 4 * (1 - parity) if ph == 0 else 4 * parity
+        loads[ph].wait()
         for m in range(MEMBERS):
-            x = nt(eye128, recv[ph, m])
-            xf[m, :, pl.ds(base, 4), :, 0:NV] = x.reshape(2, 4, 16, NV)
-
+            block = recv[ph, m]
+            both = jnp.concatenate([block * low_level, block * high_level], axis=0)
+            xf[m, pl.ds(base * 16, 64), 0 : 2 * NV] = nt(fold, both)
+
+    for load in observations:
+        load.wait()
     lane = iota((128, 128), 1)
     pad = jnp.zeros((128, 112), jnp.int32)
     spread_index = jnp.concatenate([index[0].reshape(128, 16), pad], axis=1)
     idx = jnp.take_along_axis(spread_index, lane // 8, axis=1, mode="promise_in_bounds")
-    level = idx >= NV
-    inner = jnp.where(level, idx - NV, idx)
-    upper = inner >= 128
-    inner = jnp.bitwise_and(inner, 127)
+    tile = idx // 128
+    inner = jnp.bitwise_and(idx, 127)
     slot_member = jnp.bitwise_and(lane, 7)
     observed = jnp.zeros((128, 128), F32)
     for m in range(MEMBERS):
         picks = []
-        for a in range(2):
-            for part in range(2):
-                x = xf[m, a, :, :, 128 * part : 128 * part + 128].reshape(128, 128)
-                picks.append(jnp.take_along_axis(x, inner, axis=1, mode="promise_in_bounds"))
-        got = jnp.where(
-            level,
-            jnp.where(upper, picks[3], picks[2]),
-            jnp.where(upper, picks[1], picks[0]),
-        )
+        for part in range(3):
+            x = xf[m, :, 128 * part : 128 * part + 128]
+            picks.append(jnp.take_along_axis(x, inner, axis=1, mode="promise_in_bounds"))
+        got = jnp.where(tile == 0, picks[0], jnp.where(tile == 1, picks[1], picks[2]))
         observed = jnp.where(slot_member == m, got, observed)
     obs_t = observed.T
 
@@ -571,15 +605,19 @@
     sub = iota((8, 128), 0)
     rows = [jnp.zeros((8, 128), F32) for _ in range(MEMBERS)]
     right = jnp.zeros((8, 128), F32)
+    devs = []
     for k in range(16):
         y = obs_t[8 * k : 8 * k + 8]
         mean = jnp.sum(y, axis=0, keepdims=True) * (1.0 / MEMBERS)
         dev = y - mean
+        devs.append(dev)
         r = jnp.where(live_count > k, terms[16 + k : 17 + k], 0.0)
         scaled = dev * r
         right = right + scaled * (terms[k : k + 1] - mean)
+        scaled_ref[k] = scaled
+    for k in range(16):
         for i in range(MEMBERS):
-            rows[i] = rows[i] + scaled[i : i + 1] * dev
+            rows[i] = rows[i] + scaled_ref[k, i : i + 1, :] * devs[k]
     for i in range(MEMBERS):
         rows[i] = rows[i] + jnp.where(sub == i, MEMBERS - 1.0, 0.0)
     diagonal = jnp.zeros((8, 128), F32)
@@ -589,26 +627,35 @@
     inverse_trace = 1.0 / trace
     g = [row * inverse_trace for row in rows]
 
-    def product(left, right_mat):
+    def product(slot, right_mat):
         result = []
         for i in range(MEMBERS):
-            total = left[i][0:1] * right_mat[0]
-            for j in range(1, MEMBERS):
-                total = total + left[i][j : j + 1] * right_mat[j]
-            result.append(total)
+            terms_ = [work[slot, i, j : j + 1, :] * right_mat[j] for j in range(MEMBERS)]
+            while len(terms_) > 1:
+                terms_ = [terms_[n] + terms_[n + 1] for n in range(0, len(terms_), 2)]
+            result.append(terms_[0])
         return result
+
+    def keep(slot, mat):
+        for i in range(MEMBERS):
+            work[slot, i] = mat[i]
 
     def factor_of(zg):
         return [jnp.where(sub == i, 1.5, 0.0) - 0.5 * zg[i] for i in range(MEMBERS)]
 
     f = factor_of(g)
-    g = product(g, f)
+    keep(0, g)
+    g = product(0, f)
     z = f
+    keep(1, z)
     for step in range(1, NEWTON):
-        f = factor_of(product(z, g))
+        f = factor_of(product(1, g))
+        keep(2, f)
         if step < NEWTON - 1:
-            g = product(g, f)
-        z = product(f, z)
+            keep(0, g)
+            g = product(0, f)
+        z = product(2, z)
+        keep(1, z)
 
     def apply(mat, vec):
         total = mat[0] * vec[0:1]
@@ -640,30 +687,46 @@
                 total = vt[ph, 0, m : m + 1, :] * x[0]
                 for i in range(1, MEMBERS):
                     total = total + vt[ph, i, m : m + 1, :] * x[i]
-                high = total.astype(BF16)
-                ybuf[0, ph, m, at, :] = high
-                ybuf[1, ph, m, at, :] = (total - high.astype(F32)).astype(BF16)
+                ybuf[ph, m, at, :] = total.astype(BF16)
         return 0
 
-    lax.fori_loop(0, NV // 16, update, 0)
-
-    for ph in range(2):
-        base = 4 * (1 - parity) if ph == 0 else 4 * parity
-        for m in range(MEMBERS):
-            x = nt(eye128, ybuf[0, ph, m]) + nt(eye128, ybuf[1, ph, m])
-            out[m, :, pl.ds(base, 4), :, :] = x.reshape(2, 4, 16, NV)
+    lax.fori_loop(0, NV // 16, update, 0, unroll=True)
+
+    copies = []
+    for m in range(MEMBERS):
+        for ph in range(2):
+            base = 4 * (1 - parity) if ph == 0 else 4 * parity
+            x = nt(eye128, ybuf[ph, m])
+            obuf[m, :, pl.ds(base, 4), :, :] = x.reshape(2, 4, 16, NV)
+        copy = pltpu.make_async_copy(obuf.at[m], out.at[m], out_sem.at[m])
+        copy.start()
+        copies.append(copy)
+    for copy in copies:
+        copy.wait()
 
 
 def analyse(recv, index, count, value, weight):
     return pl.pallas_call(
         analysis_kernel,
         out_shape=jax.ShapeDtypeStruct((MEMBERS, 2, 8, 16, NV), F32),
+        out_specs=pl.BlockSpec(memory_space=pl.ANY),
+        in_specs=[pl.BlockSpec(memory_space=pl.ANY)] * 5,
         scratch_shapes=[
-            pltpu.VMEM((MEMBERS, 2, 8, 16, 256), F32),
+            pltpu.VMEM((2, MEMBERS, NV, 128), BF16),
+            pltpu.VMEM((1, 8, 16, 16), jnp.int32),
+            pltpu.VMEM((1, 8, 16), jnp.int32),
+            pltpu.VMEM((1, 8, 16, 16), F32),
+            pltpu.VMEM((1, 8, 16, 16), F32),
+            pltpu.SemaphoreType.DMA((6,)),
+            pltpu.VMEM((MEMBERS, 128, 384), F32),
             pltpu.VMEM((2, MEMBERS, MEMBERS, 128), F32),
-            pltpu.VMEM((2, 2, MEMBERS, NV, 128), BF16),
+            pltpu.VMEM((2, MEMBERS, NV, 128), BF16),
+            pltpu.VMEM((MEMBERS, 2, 8, 16, NV), F32),
+            pltpu.VMEM((3, MEMBERS, MEMBERS, 128), F32),
+            pltpu.VMEM((16, MEMBERS, 128), F32),
+            pltpu.SemaphoreType.DMA((MEMBERS,)),
         ],
-        compiler_params=pltpu.CompilerParams(vmem_limit_bytes=48 * 1024 * 1024),
+        compiler_params=pltpu.CompilerParams(vmem_limit_bytes=60 * 1024 * 1024),
         cost_estimate=pl.CostEstimate(
             flops=20_000_000, bytes_accessed=3_000_000, transcendentals=0
         ),

time: 49.7 us -> 48.9 us (0.984)
  local copies, waits for them, and re-layouts: 1.1 us -> 0 us
    unnamed x10 -> x0, local copies, waits for them, and re-layouts: 1.1 us -> none
where the time goes in v2:
time: 48.9 us; the launch traced here: 48.7 us
  Pallas kernels  47.9 us (98%)
  between operations  0.82 us (2%)
    pallas_call x1, Pallas kernels, forecast(): pl.pallas_call(forecast_kernel, out_shape=jax.ShapeDtypeStruct((2, MEMBER...  42.5 us
    pallas_call x1, Pallas kernels, analyse(): pl.pallas_call(analysis_kernel, out_shape=jax.ShapeDtypeStruct((MEMBERS,...  5.46 us

profile of v2, /device:TPU:1, one launch (start us, length us, event | category | flops | bytes accessed | tf_op | source)
XLA Modules:
  0.0 48.7 jit_solution(14091765872438249447)
XLA Ops:
  0.7 42.5 %forecast.1.arrived = bf16[2,8,160,128]{3,2,1,0:T(8,128)(2,1)} custom-call(s32[1]{0:T(128)S(6)} %copy.13.off_ref, bf16[1,4,8,192,128]{4,3,2,1,0:T(8,128)(2,1)} %bitcast.4, bf16[3,192,96]{2,1,0:T(8,128)(2,1)} %bitcast.5, bf16[96,192]{1,0:T(8,128)(2,1)} %wout_in.1, bf16[192,384]{1,0:T(8,128)(2,1)} %wup_in.1, bf16[192,384]{1,0:T(8,128)(2,1)} %bitcast.6, ...), custom_call_target="tpu_custom_call" | custom-call | flops 3000000000 | bytes 6000000 | tf_op jit(solution)/shard_map/forecast/pallas_call | solution.py:475
  43.1 5.5 %analyse.1 = f32[8,2,8,16,160]{4,3,2,1,0:T(8,128)} custom-call(bf16[2,8,160,128]{3,2,1,0:T(8,128)(2,1)} %forecast.1.arrived, s32[1,8,16,16]{3,2,1,0:T(8,128)} %index_in.1, s32[1,8,16]{2,1,0:T(8,128)} %count_in.1, f32[1,8,16,16]{3,2,1,0:T(8,128)} %value_in.1, f32[1,8,16,16]{3,2,1,0:T(8,128)} %weight_in.1), custom_call_target="tpu_custom_call" | custom-call | flops 20000000 | bytes 3000000 | tf_op jit(solution)/shard_map/analyse/pallas_call | solution.py:709

commit v3 on v2

--- a/solution.py
+++ b/solution.py
@@ -208,9 +208,6 @@
     weights[0].start()
     halos[0].start()
     weights[1].start()
-    halos[1].start()
-    for i in range(2, 5):
-        weights[i].start()
 
     def prepare(block, ph, slot, keep):
         tokens = block.astype(F32)
@@ -232,6 +229,9 @@
         for r in range(4):
             prepare(jnp.concatenate([halo[ph, 0, r], halo[ph, 1, r]], axis=1), ph, 4 + r, False)
 
+    for i in range(2, 5):
+        weights[i].start()
+    halos[1].start()
     lax.fori_loop(0, 16, build_send, 0)
     for copy in locals_:
         copy.wait()
@@ -324,7 +324,7 @@
                 sbuf[w] = nn(kbuf[pl.ds(start, 128), :], jnp.concatenate(columns, axis=1))
             return 0
 
-        lax.fori_loop(begin, end, step, 0)
+        lax.fori_loop(begin, end, step, 0, unroll=5)
 
     def mlp(ph):
         def first(j):

time: 48.9 us -> 46.8 us (0.957)
  Pallas kernels: 47.9 us -> 45.9 us
    pallas_call x1, Pallas kernels: 42.5 us -> 40.4 us  [forecast(): pl.pallas_call(forecast_kernel, out_shape=jax.ShapeDtypeStruct((2, MEMBER...]
where the time goes in v3:
time: 46.8 us; the launch traced here: 46.7 us
  Pallas kernels  45.9 us (98%)
  between operations  0.82 us (2%)
    pallas_call x1, Pallas kernels, forecast(): pl.pallas_call(forecast_kernel, out_shape=jax.ShapeDtypeStruct((2, MEMBER...  40.4 us
    pallas_call x1, Pallas kernels, analyse(): pl.pallas_call(analysis_kernel, out_shape=jax.ShapeDtypeStruct((MEMBERS,...  5.45 us

profile of v3, /device:TPU:1, one launch (start us, length us, event | category | flops | bytes accessed | tf_op | source)
XLA Modules:
  0.0 46.7 jit_solution(8419056883307860754)
XLA Ops:
  0.7 40.4 %forecast.1.arrived = bf16[2,8,160,128]{3,2,1,0:T(8,128)(2,1)} custom-call(s32[1]{0:T(128)S(6)} %copy.13.off_ref, bf16[1,4,8,192,128]{4,3,2,1,0:T(8,128)(2,1)} %bitcast.4, bf16[3,192,96]{2,1,0:T(8,128)(2,1)} %bitcast.5, bf16[96,192]{1,0:T(8,128)(2,1)} %wout_in.1, bf16[192,384]{1,0:T(8,128)(2,1)} %wup_in.1, bf16[192,384]{1,0:T(8,128)(2,1)} %bitcast.6, ...), custom_call_target="tpu_custom_call" | custom-call | flops 3000000000 | bytes 6000000 | tf_op jit(solution)/shard_map/forecast/pallas_call | solution.py:475
  41.1 5.5 %analyse.1 = f32[8,2,8,16,160]{4,3,2,1,0:T(8,128)} custom-call(bf16[2,8,160,128]{3,2,1,0:T(8,128)(2,1)} %forecast.1.arrived, s32[1,8,16,16]{3,2,1,0:T(8,128)} %index_in.1, s32[1,8,16]{2,1,0:T(8,128)} %count_in.1, f32[1,8,16,16]{3,2,1,0:T(8,128)} %value_in.1, f32[1,8,16,16]{3,2,1,0:T(8,128)} %weight_in.1), custom_call_target="tpu_custom_call" | custom-call | flops 20000000 | bytes 3000000 | tf_op jit(solution)/shard_map/analyse/pallas_call | solution.py:709

commit v4 on v3

--- a/solution.py
+++ b/solution.py
@@ -279,8 +279,7 @@
     ones16 = jnp.ones((16, 128), BF16)
 
     def attend(ph, begin, end):
-        def step(i, _):
-            j = jnp.clip(i - 2, 0, 7)
+        def combine(j):
             results = []
             for w in range(2):
                 result = []
@@ -290,7 +289,7 @@
                     )
                     result.append(nn(left, pbuf[w, :, 128 * t : 128 * t + 128]))
                 results.append(result)
-            where = pl.ds(pl.multiple_of(128 * j, 128), 128)
+            where = slice(128 * j, 128 * j + 128)
             for t in range(3):
                 a, b = results[0][t], results[1][t]
                 even = jnp.where(low, a[0:32], b[0:32])
@@ -300,6 +299,7 @@
                 mixbuf[32 * t : 32 * t + 32, where] = even.astype(BF16)
                 mixbuf[96 + 32 * t : 128 + 32 * t, where] = odd.astype(BF16)
 
+        def soften():
             for w in range(2):
                 for t in range(3):
                     s = sbuf[w, :, 128 * t : 128 * t + 128] * (LOG2E * 32**-0.5)
@@ -307,7 +307,7 @@
                     s = s - jnp.max(s, axis=0, keepdims=True)
                     pbuf[w, :, 128 * t : 128 * t + 128] = jnp.exp2(s).astype(BF16)
 
-            j = jnp.minimum(i, 7)
+        def score(j):
             for w in range(2):
                 columns = []
                 for t in range(3):
@@ -320,11 +320,16 @@
                         axis=0,
                     )
                     columns.append(jnp.concatenate(pieces, axis=0))
-                start = pl.multiple_of(256 * j + 128 * w, 128)
-                sbuf[w] = nn(kbuf[pl.ds(start, 128), :], jnp.concatenate(columns, axis=1))
-            return 0
-
-        lax.fori_loop(begin, end, step, 0, unroll=5)
+                start = 256 * j + 128 * w
+                sbuf[w] = nn(kbuf[start : start + 128, :], jnp.concatenate(columns, axis=1))
+
+        for i in range(begin, end):
+            if i >= 2:
+                combine(i - 2)
+            if 1 <= i <= 8:
+                soften()
+            if i <= 7:
+                score(i)
 
     def mlp(ph):
         def first(j):

time: 46.8 us -> 45.3 us (0.968)
  Pallas kernels: 45.9 us -> 44.5 us
    pallas_call x1, Pallas kernels: 40.4 us -> 39 us  [forecast(): pl.pallas_call(forecast_kernel, out_shape=jax.ShapeDtypeStruct((2, MEMBER...]
where the time goes in v4:
time: 45.3 us; the launch traced here: 45.1 us
  Pallas kernels  44.5 us (98%)
  between operations  0.66 us (1%)
    pallas_call x1, Pallas kernels, forecast(): pl.pallas_call(forecast_kernel, out_shape=jax.ShapeDtypeStruct((2, MEMBER...  39 us
    pallas_call x1, Pallas kernels, analyse(): pl.pallas_call(analysis_kernel, out_shape=jax.ShapeDtypeStruct((MEMBERS,...  5.45 us

profile of v4, /device:TPU:1, one launch (start us, length us, event | category | flops | bytes accessed | tf_op | source)
XLA Modules:
  0.0 45.1 jit_solution(1271707666680766321)
XLA Ops:
  0.7 39.0 %forecast.1.arrived = bf16[2,8,160,128]{3,2,1,0:T(8,128)(2,1)} custom-call(s32[1]{0:T(128)S(6)} %copy.13.off_ref, bf16[1,4,8,192,128]{4,3,2,1,0:T(8,128)(2,1)} %bitcast.4, bf16[3,192,96]{2,1,0:T(8,128)(2,1)} %bitcast.5, bf16[96,192]{1,0:T(8,128)(2,1)} %wout_in.1, bf16[192,384]{1,0:T(8,128)(2,1)} %wup_in.1, bf16[192,384]{1,0:T(8,128)(2,1)} %bitcast.6, ...), custom_call_target="tpu_custom_call" | custom-call | flops 3000000000 | bytes 6000000 | tf_op jit(solution)/shard_map/forecast/pallas_call | solution.py:480
  39.7 5.5 %analyse.1 = f32[8,2,8,16,160]{4,3,2,1,0:T(8,128)} custom-call(bf16[2,8,160,128]{3,2,1,0:T(8,128)(2,1)} %forecast.1.arrived, s32[1,8,16,16]{3,2,1,0:T(8,128)} %index_in.1, s32[1,8,16]{2,1,0:T(8,128)} %count_in.1, f32[1,8,16,16]{3,2,1,0:T(8,128)} %value_in.1, f32[1,8,16,16]{3,2,1,0:T(8,128)} %weight_in.1), custom_call_target="tpu_custom_call" | custom-call | flops 20000000 | bytes 3000000 | tf_op jit(solution)/shard_map/analyse/pallas_call | solution.py:714
